TPU v7x, 256 devices: a whole 4x4x8 slice. The times are simulated.
256 devices in a mesh: dp: 8 (over y, core), tower: 2 (over z_hi), tensor: 16 (over z_lo, x).
Axes of the slice: x: 4, y: 4, z: 8 (z_hi: 2, z_lo: 4; z = z_hi * 4 + z_lo), core: 2. Of those that a mesh axis runs over, the one named last changes fastest.
Arguments:
- q_act: bfloat16 [24576, 1536], P(('dp', 'tower', 'tensor')), may hold values from -6 to 6
- q_norm_gain: bfloat16 [1536], replicated, may hold values from 0.099609375 to 1.8984375
- q_gate: bfloat16 [1536, 8960], P(None, 'tensor'), may hold values from -0.15625 to 0.15625
- q_up: bfloat16 [1536, 8960], P(None, 'tensor'), may hold values from -0.15625 to 0.15625
- q_down: bfloat16 [8960, 1536], P('tensor'), may hold values from -0.125 to 0.125
- q_final_gain: bfloat16 [1536], replicated, may hold values from 0.099609375 to 1.8984375
- projection: bfloat16 [1536, 768], replicated, may hold values from -1 to 1
- i_act: bfloat16 [8192, 768], P(('dp', 'tower', 'tensor')), may hold values from -6 to 6
- i_norm_gain: bfloat16 [768], replicated, may hold values from 0.099609375 to 1.8984375
- i_gate: bfloat16 [768, 3072], P(None, ('tower', 'tensor')), may hold values from -0.21875 to 0.21875
- i_up: bfloat16 [768, 3072], P(None, ('tower', 'tensor')), may hold values from -0.21875 to 0.21875
- i_down: bfloat16 [3072, 768], P(('tower', 'tensor')), may hold values from -0.109375 to 0.109375
- i_final_gain: bfloat16 [768], replicated, may hold values from 0.099609375 to 1.8984375
- ranks: int32 [16, 16], replicated, may hold values from 0 to 15, each once within a row
- positive: int32 [16], replicated, may hold values from 0 to 15
Outputs:
- loss_value: float32 [], replicated
- q_grad: float32 [8960, 1536], P('tensor', ('dp', 'tower'))
- i_grad: float32 [3072, 768], P(('tower', 'tensor'), 'dp')
Inputs may be any that keep to these rules, and one draw needn't show every extreme that they name: Each row of ranks holds every rank 0 to 15 once.
All inputs are finite; a program needn't handle non-finite values.
Results may differ from a plain program's by a relative error of at most 0.0012.
Values may be sent and summed in bfloat16 or wider, within the bound.
A program may use at most 128 MiB of HBM per device.

v0:
```python
import functools

import jax
import jax.numpy as jnp
from jax import lax
from jax.experimental import pallas as pl
from jax.experimental.pallas import tpu as pltpu
from jax.sharding import PartitionSpec as P

QLEN = 1536
ILEN = 512
EPS = 1e-06
TAU = 0.05
TEACH = 2.0
LOSS_SCALE = 64.0
HIGH = lax.Precision.HIGHEST
MESH = pl.DeviceIdType.MESH
F32 = jnp.float32
BF16 = jnp.bfloat16

X = 4
ZL = 4
ZR = 8
VMEM_LIMIT = 60 * 1024 * 1024


def rms_scale(values):
    return lax.rsqrt(jnp.mean(values * values, axis=-1, keepdims=True) + EPS)


def dot(left, right, dims=((1,), (0,)), precision=None):
    return lax.dot_general(
        left, right, (dims, ((), ())), preferred_element_type=F32, precision=precision
    )


def remote(src, dst, send, recv, where):
    return pltpu.make_async_remote_copy(
        src_ref=src, dst_ref=dst, send_sem=send, recv_sem=recv, device_id=where, device_id_type=MESH
    )


class Place:
    def __init__(self):
        self.t = lax.axis_index("tensor")
        self.w = lax.axis_index("tower")
        self.a = self.t // X
        self.b = self.t % X
        self.z = self.w * ZL + self.a
        self.bp = (self.b + 1) % X
        self.bm = (self.b + X - 1) % X
        self.bo = (self.b + 2) % X
        self.xp = {"tensor": self.a * X + self.bp}
        self.xm = {"tensor": self.a * X + self.bm}
        self.zp = self.ring(1)
        self.zm = self.ring(ZR - 1)

    def ring(self, step):
        z = (self.z + step) % ZR
        return {"tower": z // ZL, "tensor": (z % ZL) * X + self.b}

    def column(self, row):
        return {"tensor": row * X + self.b}

    def order(self, j):
        near = jnp.minimum(self.a, ZL - 1 - self.a)
        swapped = jnp.where(j == 0, 1, jnp.where(j == 1, 0, j))
        row = jnp.where(near == 1, swapped, j)
        return jnp.where(self.a >= 2, ZL - 1 - row, row)


def rows_of(ref, first, count, unit):
    return ref.at[pl.ds(pl.multiple_of(first, unit), count), :]


class RowGather:
    def __init__(self, place, buf, rows, send, recv):
        self.p, self.buf, self.n, self.send, self.recv = place, buf, rows, send, recv

    def block(self, s, b):
        return rows_of(self.buf, (s * X + b) * self.n, self.n, self.n)

    def half(self, s, b, h):
        n = self.n // 2
        return rows_of(self.buf, (s * X + b) * self.n + h * n, n, n)

    def up(self, s):
        ref = self.block(s, self.p.b)
        where = self.p.column(jnp.minimum(self.p.a + 1, ZL - 1))
        return remote(ref, ref, self.send.at[0, s], self.recv.at[0, s], where)

    def down(self, s):
        ref = self.block(s, self.p.b)
        where = self.p.column(jnp.maximum(self.p.a - 1, 0))
        return remote(ref, ref, self.send.at[1, s], self.recv.at[0, s], where)

    def right(self, s):
        ref = self.block(s, self.p.b)
        return remote(ref, ref, self.send.at[2, s], self.recv.at[1, s], self.p.xp)

    def left(self, s):
        ref = self.block(s, self.p.b)
        return remote(ref, ref, self.send.at[3, s], self.recv.at[2, s], self.p.xm)

    def half_right(self, s):
        ref = self.half(s, self.p.bm, 0)
        return remote(ref, ref, self.send.at[4, s], self.recv.at[3, s], self.p.xp)

    def half_left(self, s):
        ref = self.half(s, self.p.bp, 1)
        return remote(ref, ref, self.send.at[5, s], self.recv.at[4, s], self.p.xm)

    def goes_up(self, s):
        return (s <= self.p.a) & (self.p.a < ZL - 1)

    def goes_down(self, s):
        return (s >= self.p.a) & (self.p.a > 0)

    def take_z(self, s):
        @pl.when(s != self.p.a)
        def _():
            self.up(s).wait_recv()

        @pl.when(self.goes_up(s))
        def _():
            self.up(s).start()

        @pl.when(self.goes_down(s))
        def _():
            self.down(s).start()

        self.right(s).start()
        self.left(s).start()

    def take_x(self, s):
        ref = self.block(s, self.p.bm)
        remote(ref, ref, self.send.at[2, s], self.recv.at[1, s], self.p.xm).wait_recv()
        self.half_right(s).start()
        ref = self.block(s, self.p.bp)
        remote(ref, ref, self.send.at[3, s], self.recv.at[2, s], self.p.xp).wait_recv()
        self.half_left(s).start()

    def take_halves(self, s):
        ref = self.half(s, self.p.bo, 0)
        remote(ref, ref, self.send.at[4, s], self.recv.at[3, s], self.p.xm).wait_recv()
        ref = self.half(s, self.p.bo, 1)
        remote(ref, ref, self.send.at[5, s], self.recv.at[4, s], self.p.xp).wait_recv()

    def drain(self):
        def each(s, _):
            @pl.when(self.goes_up(s))
            def _():
                self.up(s).wait_send()

            @pl.when(self.goes_down(s))
            def _():
                self.down(s).wait_send()

            self.right(s).wait_send()
            self.left(s).wait_send()
            self.half_right(s).wait_send()
            self.half_left(s).wait_send()
            return 0

        lax.fori_loop(0, ZL, each, 0)


class RingGather:
    def __init__(self, place, buf, rows, send, recv):
        self.p, self.buf, self.n, self.send, self.recv = place, buf, rows, send, recv

    def ref(self, z, hop, upward):
        z = (z + 2 * ZR) % ZR
        if hop < 4:
            return rows_of(self.buf, z * self.n, self.n, self.n)
        n = self.n // 2
        return rows_of(self.buf, z * self.n + (0 if upward else n), n, n)

    def copies(self, hop):
        up = self.ref(self.p.z - hop + 1, hop, True)
        down = self.ref(self.p.z + hop - 1, hop, False)
        return (
            remote(up, up, self.send.at[0, hop - 1], self.recv.at[0, hop - 1], self.p.zp),
            remote(down, down, self.send.at[1, hop - 1], self.recv.at[1, hop - 1], self.p.zm),
        )

    def start(self, hop):
        for copy in self.copies(hop):
            copy.start()

    def take(self, hop):
        up = self.ref(self.p.z - hop, hop, True)
        down = self.ref(self.p.z + hop, hop, False)
        remote(up, up, self.send.at[0, hop - 1], self.recv.at[0, hop - 1], self.p.zm).wait_recv()
        remote(down, down, self.send.at[1, hop - 1], self.recv.at[1, hop - 1], self.p.zp).wait_recv()

    def drain(self):
        for hop in range(1, 5):
            for copy in self.copies(hop):
                copy.wait_send()


class RingSum:
    def __init__(self, place, buf, land, rows, send, recv):
        self.p, self.buf, self.land = place, buf, land
        self.n, self.send, self.recv = rows, send, recv

    def part(self, z, half):
        z = (z + 2 * ZR) % ZR
        if half is None:
            return rows_of(self.buf, z * self.n, self.n, self.n)
        n = self.n // 2
        return rows_of(self.buf, z * self.n + half * n, n, n)

    def slot(self, way, hop):
        if hop == 1:
            return self.land.at[way, 0, pl.ds(0, self.n // 2), :]
        return self.land.at[way, hop - 1]

    def copies(self, hop):
        half = (0, 1) if hop == 1 else (None, None)
        up = self.part(self.p.z + 5 - hop, half[0])
        down = self.part(self.p.z - 5 + hop, half[1])
        return (
            remote(up, self.slot(0, hop), self.send.at[0, hop - 1], self.recv.at[0, hop - 1], self.p.zp),
            remote(down, self.slot(1, hop), self.send.at[1, hop - 1], self.recv.at[1, hop - 1], self.p.zm),
        )

    def start(self, hop):
        for copy in self.copies(hop):
            copy.start()

    def take(self, hop):
        for copy in self.copies(hop):
            copy.wait_recv()

    def add(self, hop):
        half = (0, 1) if hop == 1 else (None, None)
        for way, z in ((0, self.p.z + 4 - hop), (1, self.p.z - 4 + hop)):
            ref = self.part(z, half[way])
            ref[...] = (ref[...].astype(F32) + self.slot(way, hop)[...].astype(F32)).astype(BF16)

    def drain(self):
        for hop in range(1, 5):
            for copy in self.copies(hop):
                copy.wait_send()


def gain_row(ref):
    return ref[...].astype(F32).reshape(1, -1)


def normed_rows(act, gain):
    values = act.astype(F32)
    return (values * rms_scale(values) * gain).astype(BF16)


def gated(gate_val, up_val):
    return (jax.nn.silu(gate_val) * up_val).astype(BF16)


def at_step(i, step):
    return pl.when(i == step)


def split_rows(row):
    high = row.astype(BF16).astype(F32)
    rest = row - high
    mid = rest.astype(BF16).astype(F32)
    low = rest - mid
    index = lax.broadcasted_iota(jnp.int32, (8, row.shape[1]), 0)
    out = jnp.where(index == 0, high, jnp.where(index == 1, mid, jnp.where(index == 2, low, 0.0)))
    return out.astype(BF16)


def unit_scale(vec):
    return lax.rsqrt(jnp.sum(vec * vec, axis=-1, keepdims=True) + EPS)


def unit_back(vec, scales, upstream):
    inner = jnp.sum(vec * upstream, axis=-1, keepdims=True)
    return scales * upstream - vec * (scales * scales * scales) * inner


def contrast(query_hat, item_hat, ranks, positive):
    logits = dot(query_hat, item_hat, ((1,), (1,)), HIGH) / TAU
    shifted = logits - 1.0 / TAU
    log_student = shifted - jnp.log(jnp.sum(jnp.exp(shifted), axis=1, keepdims=True))
    teach = -ranks.astype(F32) / TEACH
    log_teacher = teach - jnp.log(jnp.sum(jnp.exp(teach), axis=1, keepdims=True))
    teacher = jnp.exp(log_teacher)
    columns = lax.broadcasted_iota(jnp.int32, logits.shape, 1)
    onehot = (columns == positive).astype(F32)
    per_row = jnp.sum(
        teacher * (log_teacher - log_student) - onehot * log_student, axis=1, keepdims=True
    )
    slopes = 2.0 * jnp.exp(log_student) - onehot - teacher
    return (per_row, slopes)


def grad_rows(resid, scales, gain, upstream):
    along = gain * upstream
    inner = jnp.mean(along * resid, axis=-1, keepdims=True)
    return (scales * along - resid * (scales * scales * scales) * inner).astype(BF16)


def by_tower(values, parts, tower):
    wide = values.shape[1] // parts
    blocks = [values[:, d * wide : (d + 1) * wide] for d in range(tower, parts, 2)]
    return jnp.concatenate(blocks, axis=1)


def kernel(
    qa, qg, gate_hbm, up_hbm, down_hbm, ia, ig, ig_w, iu_w, id_w, qf, if_, proj_hbm, ranks, positive,
    loss, q_out, i_out,
    w, proj, nq, part, gate_val, h2, pm, r1, r2, zs, zin, ni, wi, ip, land, hq, hi,
    sums, hats, scal, yq, grad, yi, gq, gi, qc1, qb1, qb2, qc, ic1, ib1, ib2, ic,
    loads, gs, gr, ss, sr, ws, wr, vs, vr, hs, hr, ias, iar, irs, irr,
    s1, r1s, s2, r2s, s3, r3s, ys, yr, iys, iyr, qs, qv, bs, bv,
):
    p = Place()
    n, dq = qa.shape
    m, di = ia.shape
    f, k = down_hbm.shape[0], id_w.shape[0]
    group = X * n
    h = n // 2
    parts = X * ZL
    count = hats.shape[0]
    block_wide = dq // count
    piece = w.shape[2] // 4
    wide, thin = dq // 2, dq // 4
    dp = lax.axis_index("dp")
    own = dp * 2 + p.w
    y, c = dp // 2, dp % 2
    yp, ym, y2 = (y + 1) % 4, (y + 3) % 4, (y + 2) % 4
    line_y = (y2, yp, ym, y)
    to_yp, to_ym, to_core = {"dp": yp * 2 + c}, {"dp": ym * 2 + c}, {"dp": y * 2 + 1 - c}
    to_y = (to_yp, to_ym)
    to_tower = {"tower": 1 - p.w}
    a2 = (p.a + 2) % ZL
    mate = p.a + 1 - 2 * (p.a % 2)
    to_a2, to_mate = p.column(a2), p.column(mate)

    def member(step):
        return {"tensor": (p.t + step) % parts}

    def replica(step):
        other = (own + step) % count
        return {"dp": other // 2, "tower": other % 2}

    own_weights = [
        pltpu.make_async_copy(ref, w.at[0, index, pl.ds(0, f), :], loads.at[index])
        for index, ref in enumerate((gate_hbm, up_hbm, down_hbm))
    ]
    proj_copy = pltpu.make_async_copy(proj_hbm, proj, loads.at[3])
    for copy in own_weights:
        copy.start()
    proj_copy.start()
    barrier = pltpu.get_barrier_semaphore()

    def greet(step, _):
        pl.semaphore_signal(barrier, inc=1, device_id=member(step), device_id_type=MESH)
        pl.semaphore_signal(barrier, inc=1, device_id=replica(step), device_id_type=MESH)
        return 0

    lax.fori_loop(1, parts, greet, 0)
    for where in (p.zp, p.zm):
        pl.semaphore_signal(barrier, inc=1, device_id=where, device_id_type=MESH)
    for index in range(3):
        w[0, index, f:, :] = jnp.zeros((w.shape[2] - f, dq), BF16)
    nq[pl.ds(pl.multiple_of(p.b * n, n), n), :] = normed_rows(qa[...], gain_row(qg))
    ni[pl.ds(pl.multiple_of(p.z * m, m), m), :] = normed_rows(ia[...], gain_row(ig))
    for index, ref in enumerate((ig_w, iu_w, id_w)):
        wi[index, pl.ds(pl.multiple_of(p.b * k, k), k), :] = ref[...]
    pl.semaphore_wait(barrier, 2 * (parts - 1) + 2)

    rows = RowGather(p, nq, n, gs, gr)
    items = RingGather(p, ni, m, ias, iar)
    isum = RingSum(p, ip, land, m, irs, irr)

    def across():
        return remote(rows.block(0, p.b), rows.block(1, p.b), gs.at[0, 0], gr.at[0, 0], to_a2)

    def wpiece(which, index, line, core):
        first = pl.multiple_of(line * piece, piece)
        return w.at[which, index, pl.ds(first, piece), pl.ds(pl.multiple_of(core * wide, wide), wide)]

    def whalf(index, line, part_of):
        first = pl.multiple_of(line * piece, piece)
        column = pl.multiple_of(c * wide + part_of * thin, thin)
        return w.at[1, index, pl.ds(first, piece), pl.ds(column, thin)]

    def w_send(index, kind):
        here = wpiece(1, index, y, c)
        low, high = wpiece(1, index, ym, c), wpiece(1, index, yp, c)
        src, dst, where = (
            (wpiece(0, index, y, c), here, to_mate),
            (here, here, to_yp),
            (here, here, to_ym),
            (whalf(index, ym, 0), whalf(index, ym, 0), to_yp),
            (whalf(index, yp, 1), whalf(index, yp, 1), to_ym),
            (here, here, to_core),
            (low, low, to_core),
            (high, high, to_core),
            (wpiece(1, index, y2, c), wpiece(1, index, y2, c), to_core),
        )[kind]
        return remote(src, dst, ws.at[kind, index], wr.at[kind, index], where)

    def w_got(index, kind):
        dst = (
            wpiece(1, index, y, c),
            wpiece(1, index, ym, c),
            wpiece(1, index, yp, c),
            whalf(index, y2, 0),
            whalf(index, y2, 1),
            wpiece(1, index, y, 1 - c),
            wpiece(1, index, ym, 1 - c),
            wpiece(1, index, yp, 1 - c),
            wpiece(1, index, y2, 1 - c),
        )[kind]
        remote(dst, dst, ws.at[kind, index], wr.at[kind, index], to_core).wait_recv()

    def w_near(index):
        w_got(index, 0)
        for kind in (1, 2, 5):
            w_send(index, kind).start()

    def w_ring(index):
        w_got(index, 1)
        w_send(index, 3).start()
        w_send(index, 6).start()
        w_got(index, 2)
        w_send(index, 4).start()
        w_send(index, 7).start()

    def w_far(index):
        w_got(index, 3)
        w_got(index, 4)
        w_send(index, 8).start()

    def w_done(index):
        for kind in (5, 6, 7, 8):
            w_got(index, kind)

    def vpiece(b, core):
        column = pl.multiple_of(core * (di // 2), di // 2)
        return wi.at[:, pl.ds(pl.multiple_of(b * k, k), k), pl.ds(column, di // 2)]

    def vhalf(b, part_of):
        first = pl.multiple_of(b * k + part_of * (k // 2), k // 2)
        column = pl.multiple_of(c * (di // 2), di // 2)
        return wi.at[:, pl.ds(first, k // 2), pl.ds(column, di // 2)]

    def v_send(kind):
        ref, where = (
            (vpiece(p.b, c), p.xp),
            (vpiece(p.b, c), p.xm),
            (vhalf(p.bm, 0), p.xp),
            (vhalf(p.bp, 1), p.xm),
            (vpiece(p.bm, c), to_core),
            (vpiece(p.bp, c), to_core),
            (vpiece(p.bo, c), to_core),
        )[kind]
        return remote(ref, ref, vs.at[kind], vr.at[kind], where)

    def v_got(kind):
        ref = (
            vpiece(p.bm, c),
            vpiece(p.bp, c),
            vhalf(p.bo, 0),
            vhalf(p.bo, 1),
            vpiece(p.bm, 1 - c),
            vpiece(p.bp, 1 - c),
            vpiece(p.bo, 1 - c),
        )[kind]
        remote(ref, ref, vs.at[kind], vr.at[kind], to_core).wait_recv()

    def block(j, q, b):
        return rows_of(pm.at[q], (j * X + b) * n, n, n)

    def half(j, q, b, part_of):
        return rows_of(pm.at[q], (j * X + b) * n + part_of * h, h, h)

    def first(j, q, way):
        src = half(j, q, p.bo, way)
        where = (p.xp, p.xm)[way]
        return remote(src, r1.at[way, j, q], ss.at[way, j, q], sr.at[way, j, q], where)

    def second(j, q, way):
        src = block(j, q, (p.bp, p.bm)[way])
        where = (p.xp, p.xm)[way]
        return remote(src, r2.at[way, j, q], ss.at[2 + way, j, q], sr.at[2 + way, j, q], where)

    def to_owner(q):
        return remote(zs.at[q], zin.at[q], ss.at[4, 0, q], sr.at[4, 0, q], to_a2)

    def back(j):
        s = (p.a, a2)[j]
        dst = hq.at[pl.ds(pl.multiple_of(s * group, group), group), :]
        return remote(h2.at[j], dst, hs.at[j], hr.at[j], to_mate)

    def back_got(j):
        other = (mate, (mate + 2) % ZL)[j]
        dst = hq.at[pl.ds(pl.multiple_of(other * group, group), group), :]
        remote(h2.at[j], dst, hs.at[j], hr.at[j], to_mate).wait_recv()

    def rows_in(j):
        return nq[j * group : (j + 1) * group, :]

    def own_units(j):
        left = rows_in(j)
        value = gated(
            dot(left, w[0, 0, :f, :], ((1,), (1,))), dot(left, w[0, 1, :f, :], ((1,), (1,)))
        )
        hq[pl.ds(pl.multiple_of((p.a, a2)[j] * group, group), group), :] = value
        part[j] = dot(value, w[0, 2, :f, :])

    def mate_gate(j):
        gate_val[j] = dot(rows_in(j), w[1, 0, :f, :], ((1,), (1,)))

    def mate_up(j):
        h2[j] = gated(gate_val[j], dot(rows_in(j), w[1, 1, :f, :], ((1,), (1,))))
        back(j).start()

    def mate_down(j, q):
        columns = slice(q * wide, (q + 1) * wide)
        total = part[j, :, columns] + dot(h2[j], w[1, 2, :f, columns])
        pm[q, j * group : (j + 1) * group, :] = total.astype(BF16)
        first(j, q, 0).start()
        first(j, q, 1).start()

    def combine(j, q):
        for way in range(2):
            first(j, q, way).wait_recv()
            ref = half(j, q, (p.bp, p.bm)[way], way)
            ref[...] = (ref[...].astype(F32) + r1[way, j, q].astype(F32)).astype(BF16)
            second(j, q, way).start()

    def summed(j, q):
        second(j, q, 0).wait_recv()
        second(j, q, 1).wait_recv()
        total = block(j, q, p.b)[...].astype(F32)
        return total + r2[0, j, q].astype(F32) + r2[1, j, q].astype(F32)

    def send_sum(q):
        zs[q] = summed(1, q).astype(BF16)
        to_owner(q).start()

    def item_hop(hop):
        items.take(hop)
        if hop < 4:
            items.start(hop + 1)

    def isum_hop(hop):
        isum.take(hop)
        isum.add(hop)
        isum.start(hop + 1)

    def item_product():
        left = ni[...]
        partial = 0.0
        for b in range(X):
            here = slice(b * k, (b + 1) * k)
            value = gated(
                dot(left, wi[0, here, :], ((1,), (1,))), dot(left, wi[1, here, :], ((1,), (1,)))
            )
            hi[b] = value
            partial = partial + dot(value, wi[2, here, :])
        ip[...] = partial.astype(BF16)
        isum.start(1)

    rows.right(0).start()
    rows.left(0).start()
    items.start(1)
    own_weights[0].wait()
    w_send(0, 0).start()
    across().start()
    v_send(0).start()
    v_send(1).start()
    own_weights[1].wait()
    own_weights[2].wait()
    rows.take_x(0)
    item_hop(1)
    w_near(0)
    w_send(1, 0).start()
    rows.take_halves(0)
    own_units(0)
    remote(rows.block(0, p.b), rows.block(1, p.b), gs.at[0, 0], gr.at[0, 0], to_a2).wait_recv()
    rows.right(1).start()
    rows.left(1).start()
    item_hop(2)
    w_ring(0)
    w_near(1)
    w_send(2, 0).start()
    for kind in range(2):
        v_got(kind)
        v_send(2 + kind).start()
        v_send(4 + kind).start()
    item_hop(3)
    w_far(0)
    rows.take_x(1)
    v_got(2)
    v_got(3)
    v_send(6).start()
    w_ring(1)
    item_hop(4)
    for kind in (4, 5, 6):
        v_got(kind)
    w_near(2)
    item_product()
    w_far(1)
    w_done(0)
    mate_gate(0)
    rows.take_halves(1)
    mate_gate(1)
    isum_hop(1)
    w_ring(2)
    own_units(1)
    w_done(1)
    mate_up(1)
    isum_hop(2)
    w_far(2)
    mate_up(0)
    w_done(2)
    mate_down(1, 0)
    mate_down(1, 1)
    combine(1, 0)
    mate_down(0, 0)
    combine(1, 1)
    mate_down(0, 1)
    isum_hop(3)
    send_sum(0)
    combine(0, 0)
    send_sum(1)
    combine(0, 1)
    isum.take(4)
    own_item = ip[pl.ds(pl.multiple_of(p.z * m, m), m), :].astype(F32)
    i_resid = ia[...].astype(F32) + (own_item + land[0, 3].astype(F32) + land[1, 3].astype(F32))
    mlp = []
    for q in range(2):
        total = summed(0, q)
        to_owner(q).wait_recv()
        mlp.append(total + zin[q].astype(F32))
    q_resid = qa[...].astype(F32) + jnp.concatenate(mlp, axis=1)

    q_gain, i_gain = gain_row(qf), gain_row(if_)
    q_scale, i_scale = rms_scale(q_resid), rms_scale(i_resid)
    sums[p.t, :, :dq] = jnp.sum(q_resid * q_scale * q_gain, axis=0, keepdims=True)
    sums[p.t, :, dq:] = jnp.sum(i_resid * i_scale * i_gain, axis=0, keepdims=True)

    def spread_members(buf, send, recv):
        def each(step, _):
            remote(buf.at[p.t], buf.at[p.t], send.at[step], recv.at[p.t], member(step)).start()
            return 0

        lax.fori_loop(1, parts, each, 0)

    def await_members(buf, send, recv):
        def each(step, _):
            other = (p.t + step) % parts
            remote(buf.at[p.t], buf.at[other], send.at[step], recv.at[other], member(step)).wait()
            return 0

        lax.fori_loop(1, parts, each, 0)

    def spread_hats(step, _):
        remote(hats.at[own], hats.at[own], s2.at[step], r2s.at[own], replica(step)).start()
        return 0

    def gathered_hats(step, _):
        other = (own + step) % count
        remote(hats.at[own], hats.at[other], s2.at[step], r2s.at[other], replica(step)).wait()
        return 0

    def q_rows(tower, line_of, core):
        return rows_of(gq.at[tower], (line_of * 2 + core) * block_wide, block_wide, block_wide)

    def q_half(tower, line_of, way):
        first = (line_of * 2 + c) * block_wide + way * (block_wide // 2)
        return rows_of(gq.at[tower], first, block_wide // 2, block_wide // 2)

    def q_core(tower, j):
        src = q_rows(tower, line_y[j], 1 - c)
        return remote(src, qc1.at[tower, j], qs.at[tower, j], qv.at[tower, j], to_core)

    def q_first(tower, way):
        src, dst = q_half(tower, y2, way), qb1.at[tower, way]
        return remote(src, dst, qs.at[tower, 4 + way], qv.at[tower, 4 + way], to_y[way])

    def q_second(tower, way):
        src, dst = q_rows(tower, (yp, ym)[way], c), qb2.at[tower, way]
        return remote(src, dst, qs.at[tower, 6 + way], qv.at[tower, 6 + way], to_y[way])

    def q_tower(tower):
        return remote(q_rows(tower, y, c), qc, qs.at[tower, 8], qv.at[tower, 8], to_tower)

    def q_start(tower):
        for j in range(4):
            q_core(tower, j).start()

    def q_far(tower):
        q_core(tower, 0).wait_recv()
        ref = q_rows(tower, y2, c)
        ref[...] += qc1[tower, 0]
        for way in range(2):
            q_first(tower, way).start()

    def q_near(tower):
        for way in range(2):
            q_core(tower, 1 + way).wait_recv()
            ref = q_rows(tower, (yp, ym)[way], c)
            ref[...] += qc1[tower, 1 + way]
            q_first(tower, way).wait_recv()
            ref = q_half(tower, (yp, ym)[way], way)
            ref[...] += qb1[tower, way]
            q_second(tower, way).start()

    def q_own(tower):
        q_core(tower, 3).wait_recv()
        for way in range(2):
            q_second(tower, way).wait_recv()
        ref = q_rows(tower, y, c)
        ref[...] = ref[...] + qc1[tower, 3] + qb2[tower, 0] + qb2[tower, 1]

        @pl.when(p.w != tower)
        def _():
            q_tower(tower).start()

    def q_finish(tower):
        @pl.when(p.w == tower)
        def _():
            q_tower(tower).wait_recv()
            q_out[...] = q_rows(tower, y, c)[...] + qc[...]

    def i_rows(line_of, core):
        first = pl.multiple_of((line_of * 2 + core) * block_wide, block_wide)
        return gi.at[:, pl.ds(first, block_wide), :]

    def i_half(line_of, way):
        first = pl.multiple_of((line_of * 2 + c) * block_wide, block_wide)
        return gi.at[pl.ds(way * 2, 2), pl.ds(first, block_wide), :]

    def i_slab(b):
        return gi.at[b, pl.ds(pl.multiple_of((y * 2 + c) * block_wide, block_wide), block_wide), :]

    def i_core(j):
        return remote(i_rows(line_y[j], 1 - c), ic1.at[j], bs.at[j], bv.at[j], to_core)

    def i_first(way):
        return remote(i_half(y2, way), ib1.at[way], bs.at[4 + way], bv.at[4 + way], to_y[way])

    def i_second(way):
        src = i_rows((yp, ym)[way], c)
        return remote(src, ib2.at[way], bs.at[6 + way], bv.at[6 + way], to_y[way])

    def i_x(hop):
        other = (p.b + hop) % X
        where = {"tensor": p.a * X + other}
        return remote(i_slab(other), ic.at[p.b], bs.at[8 + hop], bv.at[8 + p.b], where)

    def i_product():
        for b in range(X):
            gi[b] = dot(yi[...], hi[b], ((0,), (0,)))
        for j in range(4):
            i_core(j).start()

    def i_far():
        for j in range(4):
            i_core(j).wait_recv()
            ref = i_rows(line_y[j], c)
            ref[...] += ic1[j]
        for way in range(2):
            i_first(way).start()

    def i_near():
        for way in range(2):
            i_first(way).wait_recv()
            ref = i_half((yp, ym)[way], way)
            ref[...] += ib1[way]
            i_second(way).start()

    def i_own():
        for way in range(2):
            i_second(way).wait_recv()
        ref = i_rows(y, c)
        ref[...] = ref[...] + ib2[0] + ib2[1]
        for hop in range(1, X):
            i_x(hop).start()

    def i_finish():
        total = i_slab(p.b)[...]
        for hop in range(1, X):
            other = (p.b + hop) % X
            remote(i_slab(other), ic.at[other], bs.at[8 + hop], bv.at[8 + other], p.xp).wait_recv()
            total = total + ic[other]
        i_out[...] = total

    gather = [RowGather(p, yq.at[tower], n, ys.at[tower], yr.at[tower]) for tower in range(2)]
    igather = RingGather(p, yi, m, iys, iyr)

    def take_z(g):
        gather[g // ZL].take_z(p.order(g % ZL))

    def take_x(g):
        gather[g // ZL].take_x(p.order(g % ZL))

    def item_grad_hop(hop):
        igather.take(hop)
        if hop < 4:
            igather.start(hop + 1)

    def product(g):
        tower = g // ZL
        s = p.order(g % ZL)
        gather[tower].take_halves(s)
        for b in range(X):
            tile = scal[s * X + b]
            columns = jnp.concatenate([tile] * 16, axis=0).T[:n]
            first_row = pl.multiple_of((s * X + b) * n, n)
            resid = yq[tower, pl.ds(first_row, n), :].astype(F32)
            value = columns[:, 0:1] * along_of[tower] - resid * columns[:, 1:2]
            grad[b * n : (b + 1) * n, :] = value.astype(BF16)
        here = pl.ds(pl.multiple_of(s * group, group), group)
        value = dot(grad[...], hq[here, :], ((0,), (0,)))
        gq[tower] = value if g % ZL == 0 else gq[tower] + value

    spread_members(sums, s1, r1s)
    for tower in range(2):
        here = pl.ds(pl.multiple_of(p.t * n, n), n)
        yq[tower, here, :] = by_tower(q_resid, count, tower).astype(BF16)
    take_z(0)
    proj_copy.wait()
    await_members(sums, s1, r1s)
    total = sums[0]
    for slot in range(1, parts):
        total = total + sums[slot]
    q_pooled = total[:, :dq] / QLEN
    i_pooled = total[:, dq:] / ILEN
    q_e = jnp.sum(dot(split_rows(q_pooled), proj[...]), axis=0, keepdims=True)
    q_norm, i_norm = unit_scale(q_e), unit_scale(i_pooled)
    hats[own, :, :di] = q_e * q_norm
    hats[own, :, di:] = i_pooled * i_norm
    lax.fori_loop(1, count, spread_hats, 0)
    take_z(1)
    take_z(4)
    take_x(0)
    lax.fori_loop(1, count, gathered_hats, 0)
    index = lax.broadcasted_iota(jnp.int32, (count, 2 * di), 0)
    every = jnp.zeros((count, 2 * di), F32)
    for slot in range(count):
        every = jnp.where(index == slot, hats[slot], every)
    every_query, every_items = every[:, :di], every[:, di:]
    line = lax.broadcasted_iota(jnp.int32, (count, count), 0)
    target = jnp.zeros((count, count), jnp.int32)
    for slot in range(count):
        target = jnp.where(line == slot, positive[slot], target)
    per_row, slopes = contrast(every_query, every_items, ranks[...], target)
    loss[...] = jnp.sum(per_row, axis=0, keepdims=True) / count
    weights = slopes * (LOSS_SCALE / (TAU * count))
    take_z(2)
    take_x(1)
    mine = lax.broadcasted_iota(jnp.int32, (count, di), 0) == own
    q_back = jnp.sum(
        jnp.where(mine, dot(weights, every_items, precision=HIGH), 0.0), axis=0, keepdims=True
    )
    column = lax.broadcasted_iota(jnp.int32, (count, count), 1) == own
    i_back = jnp.sum(
        jnp.sum(jnp.where(column, weights, 0.0), axis=1, keepdims=True) * every_query,
        axis=0,
        keepdims=True,
    )
    q_grad_e = unit_back(q_e, q_norm, q_back)
    q_up = jnp.sum(dot(split_rows(q_grad_e), proj[...], ((1,), (1,))), axis=0, keepdims=True) / QLEN
    i_up = unit_back(i_pooled, i_norm, i_back) / ILEN
    along = q_gain * q_up
    along_of = [by_tower(along, count, tower) for tower in range(2)]
    inner = jnp.mean(along * q_resid, axis=-1, keepdims=True)
    slope = (q_scale * q_scale * q_scale) * inner
    lane = lax.broadcasted_iota(jnp.int32, (n, 128), 1)
    columns = jnp.where(lane == 0, q_scale, jnp.where(lane == 1, slope, 0.0))
    columns = jnp.concatenate([columns, jnp.zeros((128 - n, 128), F32)], axis=0)
    scal[p.t] = columns.T[:8]
    spread_members(scal, s3, r3s)
    yi[pl.ds(pl.multiple_of(p.z * m, m), m), :] = grad_rows(i_resid, i_scale, i_gain, i_up)
    igather.start(1)
    take_z(3)
    take_x(4)
    item_grad_hop(1)
    await_members(scal, s3, r3s)
    back_got(0)
    back_got(1)
    product(0)
    take_z(5)
    take_x(2)
    product(1)
    item_grad_hop(2)
    take_z(6)
    take_x(3)
    product(2)
    take_z(7)
    item_grad_hop(3)
    product(3)
    q_start(0)
    take_x(5)
    q_far(0)
    product(4)
    item_grad_hop(4)
    take_x(6)
    q_near(0)
    i_product()
    product(5)
    take_x(7)
    i_far()
    product(6)
    q_own(0)
    i_near()
    product(7)
    q_start(1)
    q_far(1)
    i_own()
    q_near(1)
    i_finish()
    q_finish(0)
    q_own(1)
    q_finish(1)

    for j in range(2):
        back(j).wait_send()
        for copy in (rows.right(j), rows.left(j), rows.half_right(j), rows.half_left(j)):
            copy.wait_send()
        for q in range(2):
            for way in range(2):
                first(j, q, way).wait_send()
                second(j, q, way).wait_send()
    for q in range(2):
        to_owner(q).wait_send()
    across().wait_send()
    items.drain()
    isum.drain()
    for index in range(3):
        for kind in range(9):
            w_send(index, kind).wait_send()
    for kind in range(7):
        v_send(kind).wait_send()
    for tower in range(2):
        gather[tower].drain()
        for j in range(4):
            q_core(tower, j).wait_send()
        for way in range(2):
            q_first(tower, way).wait_send()
            q_second(tower, way).wait_send()

        @pl.when(p.w != tower)
        def _():
            q_tower(tower).wait_send()

    igather.drain()
    for j in range(4):
        i_core(j).wait_send()
    for way in range(2):
        i_first(way).wait_send()
        i_second(way).wait_send()
    for hop in range(1, X):
        i_x(hop).wait_send()


def step(qa, qg, gate, up, down, ia, ig, ig_w, iu_w, id_w, qf, if_, proj, ranks, positive):
    n, dq = qa.shape
    m, di = ia.shape
    f, k = down.shape[0], id_w.shape[0]
    padded = 64 * ((f + 63) // 64)
    vmem, hbm = pl.BlockSpec(memory_space=pltpu.VMEM), pl.BlockSpec(memory_space=pl.ANY)
    smem = pl.BlockSpec(memory_space=pltpu.SMEM)
    all_i = ZR * m
    group = X * n
    parts = X * ZL
    count = ranks.shape[0]
    wide = dq // count
    dma = pltpu.SemaphoreType.DMA
    return pl.pallas_call(
        kernel,
        out_shape=(
            jax.ShapeDtypeStruct((1, 1), F32),
            jax.ShapeDtypeStruct((wide, f), F32),
            jax.ShapeDtypeStruct((wide, k), F32),
        ),
        in_specs=[vmem, vmem, hbm, hbm, hbm] + [vmem] * 7 + [hbm, vmem, smem],
        out_specs=[vmem] * 3,
        scratch_shapes=[
            pltpu.VMEM((2, 3, padded, dq), BF16),
            pltpu.VMEM(proj.shape, BF16),
            pltpu.VMEM((2 * group, dq), BF16),
            pltpu.VMEM((2, group, dq), F32),
            pltpu.VMEM((2, group, f), F32),
            pltpu.VMEM((2, group, f), BF16),
            pltpu.VMEM((2, 2 * group, dq // 2), BF16),
            pltpu.VMEM((2, 2, 2, n // 2, dq // 2), BF16),
            pltpu.VMEM((2, 2, 2, n, dq // 2), BF16),
            pltpu.VMEM((2, n, dq // 2), BF16),
            pltpu.VMEM((2, n, dq // 2), BF16),
            pltpu.VMEM((all_i, di), BF16),
            pltpu.VMEM((3, X * k, di), BF16),
            pltpu.VMEM((all_i, di), BF16),
            pltpu.VMEM((2, 4, m, di), BF16),
            pltpu.VMEM((ZL * group, f), BF16),
            pltpu.VMEM((X, all_i, k), BF16),
            pltpu.VMEM((parts, 1, dq + di), F32),
            pltpu.VMEM((count, 1, 2 * di), F32),
            pltpu.VMEM((parts, 8, 128), F32),
            pltpu.VMEM((2, parts * n, dq // 2), BF16),
            pltpu.VMEM((group, dq // 2), BF16),
            pltpu.VMEM((all_i, di), BF16),
            pltpu.VMEM((2, dq // 2, f), F32),
            pltpu.VMEM((X, di, k), F32),
            pltpu.VMEM((2, 4, wide, f), F32),
            pltpu.VMEM((2, 2, wide // 2, f), F32),
            pltpu.VMEM((2, 2, wide, f), F32),
            pltpu.VMEM((wide, f), F32),
            pltpu.VMEM((4, X, wide, k), F32),
            pltpu.VMEM((2, 2, wide, k), F32),
            pltpu.VMEM((2, X, wide, k), F32),
            pltpu.VMEM((X, wide, k), F32),
            dma((4,)),
            dma((6, 2)),
            dma((5, 2)),
            dma((5, 2, 2)),
            dma((5, 2, 2)),
            dma((9, 3)),
            dma((9, 3)),
            dma((7,)),
            dma((7,)),
            dma((2,)),
            dma((2,)),
            dma((2, 4)),
            dma((2, 4)),
            dma((2, 4)),
            dma((2, 4)),
            dma((parts,)),
            dma((parts,)),
            dma((count,)),
            dma((count,)),
            dma((parts,)),
            dma((parts,)),
            dma((2, 6, ZL)),
            dma((2, 5, ZL)),
            dma((2, 4)),
            dma((2, 4)),
            dma((2, 9)),
            dma((2, 9)),
            dma((12,)),
            dma((12,)),
        ],
        compiler_params=pltpu.CompilerParams(
            collective_id=0, has_side_effects=True, vmem_limit_bytes=VMEM_LIMIT
        ),
        name="towers_step",
    )(qa, qg, gate, up, down, ia, ig, ig_w, iu_w, id_w, qf, if_, proj, ranks, positive)


def body(
    q_act,
    q_norm_gain,
    q_gate,
    q_up,
    q_down,
    q_final_gain,
    projection,
    i_act,
    i_norm_gain,
    i_gate,
    i_up,
    i_down,
    i_final_gain,
    ranks,
    positive,
):
    loss, q_grad, i_grad = step(
        q_act,
        q_norm_gain,
        q_gate.T,
        q_up.T,
        q_down,
        i_act,
        i_norm_gain,
        i_gate.T,
        i_up.T,
        i_down,
        q_final_gain,
        i_final_gain,
        projection,
        ranks,
        positive,
    )
    return (loss.reshape(()), q_grad.T, i_grad.T)


def solution(mesh):
    in_specs = (
        P(("dp", "tower", "tensor"), None),
        P(),
        P(None, "tensor"),
        P(None, "tensor"),
        P("tensor", None),
        P(),
        P(),
        P(("dp", "tower", "tensor"), None),
        P(),
        P(None, ("tower", "tensor")),
        P(None, ("tower", "tensor")),
        P(("tower", "tensor"), None),
        P(),
        P(),
        P(),
    )
    out_specs = (P(), P("tensor", ("dp", "tower")), P(("tower", "tensor"), "dp"))
    return jax.shard_map(body, mesh=mesh, in_specs=in_specs, out_specs=out_specs, check_vma=False)
```

profile of v0, /device:TPU:1, one launch (start us, length us, event | category | flops | bytes accessed | tf_op | source)
XLA Modules:
  0.0 176.7 jit_solution(2420749746405776438)
XLA Ops:
  0.6 171.1 %towers_step.1 = (f32[1,1]{1,0:T(1,128)}, f32[96,560]{1,0:T(8,128)}, f32[96,96]{1,0:T(8,128)}) custom-call(bf16[96,1536]{1,0:T(8,128)(2,1)} %qa.1, bf16[1536]{0:T(1024)(128)(2,1)} %qg.1, bf16[560,1536]{1,0:T(8,128)(2,1)} %bitcast.7, bf16[560,1536]{1,0:T(8,128)(2,1)} %bitcast.8, bf16[560,1536]{1,0:T(8,128)(2,1)} %down_hbm.1, bf16[32,768]{1,0:T(8,128)(2,1)} %ia.1, ...), custom_call_target="tpu_custom_call" | custom-call | tf_op jit(solution)/shard_map/towers_step/pallas_call | solution.py:980
  171.7 1.5 copy.18
  173.9 1.7 copy.22
where the time goes:
time: 178 us; the launch traced here: 177 us
  Pallas kernels  171 us (96%)
  local copies, waits for them, and re-layouts  3.16 us (2%)
  between operations  2.47 us (1%)
    pallas_call x1, Pallas kernels, step(): pl.pallas_call(kernel, out_shape=(jax.ShapeDtypeStruct((1, 1), F32), jax....  171 us

commit v1 on v0

--- a/solution.py
+++ b/solution.py
@@ -520,7 +520,6 @@
 
     def mate_up(j):
         h2[j] = gated(gate_val[j], dot(rows_in(j), w[1, 1, :f, :], ((1,), (1,))))
-        back(j).start()
 
     def mate_down(j, q):
         columns = slice(q * wide, (q + 1) * wide)
@@ -575,64 +574,66 @@
     own_weights[0].wait()
     w_send(0, 0).start()
     across().start()
+    own_weights[1].wait()
+    own_weights[2].wait()
+    w_near(0)
+    w_send(1, 0).start()
+    rows.take_x(0)
+    item_hop(1)
     v_send(0).start()
     v_send(1).start()
-    own_weights[1].wait()
-    own_weights[2].wait()
-    rows.take_x(0)
-    item_hop(1)
-    w_near(0)
-    w_send(1, 0).start()
     rows.take_halves(0)
     own_units(0)
-    remote(rows.block(0, p.b), rows.block(1, p.b), gs.at[0, 0], gr.at[0, 0], to_a2).wait_recv()
-    rows.right(1).start()
-    rows.left(1).start()
     item_hop(2)
     w_ring(0)
     w_near(1)
     w_send(2, 0).start()
+    remote(rows.block(0, p.b), rows.block(1, p.b), gs.at[0, 0], gr.at[0, 0], to_a2).wait_recv()
+    rows.right(1).start()
+    rows.left(1).start()
+    item_hop(3)
+    w_far(0)
     for kind in range(2):
         v_got(kind)
         v_send(2 + kind).start()
         v_send(4 + kind).start()
-    item_hop(3)
-    w_far(0)
-    rows.take_x(1)
+    item_hop(4)
+    w_ring(1)
+    w_near(2)
+    w_done(0)
+    mate_gate(0)
     v_got(2)
     v_got(3)
     v_send(6).start()
-    w_ring(1)
-    item_hop(4)
+    w_far(1)
     for kind in (4, 5, 6):
         v_got(kind)
-    w_near(2)
     item_product()
-    w_far(1)
-    w_done(0)
-    mate_gate(0)
+    rows.take_x(1)
+    w_done(1)
+    mate_up(0)
+    w_ring(2)
+    isum_hop(1)
     rows.take_halves(1)
-    mate_gate(1)
-    isum_hop(1)
-    w_ring(2)
     own_units(1)
-    w_done(1)
-    mate_up(1)
     isum_hop(2)
     w_far(2)
-    mate_up(0)
+    mate_gate(1)
+    mate_up(1)
+    isum_hop(3)
     w_done(2)
+    mate_down(0, 0)
+    mate_down(0, 1)
     mate_down(1, 0)
     mate_down(1, 1)
+    back(0).start()
     combine(1, 0)
-    mate_down(0, 0)
     combine(1, 1)
-    mate_down(0, 1)
-    isum_hop(3)
+    combine(0, 0)
     send_sum(0)
-    combine(0, 0)
+    combine(0, 1)
     send_sum(1)
-    combine(0, 1)
+    back(1).start()
     isum.take(4)
     own_item = ip[pl.ds(pl.multiple_of(p.z * m, m), m), :].astype(F32)
     i_resid = ia[...].astype(F32) + (own_item + land[0, 3].astype(F32) + land[1, 3].astype(F32))

time: 178 us -> 183 us (1.028); the launches traced: 177 us -> 179 us
  Pallas kernels: 171 us -> 173 us
    pallas_call x1, Pallas kernels: 171 us -> 173 us  [step(): pl.pallas_call(kernel, out_shape=(jax.ShapeDtypeStruct((1, 1), F32), jax....]
where the time goes in v1:
time: 183 us; the launch traced here: 179 us
  Pallas kernels  173 us (95%)
  local copies, waits for them, and re-layouts  3.16 us (2%)
  between operations  2.47 us (1%)
    pallas_call x1, Pallas kernels, step(): pl.pallas_call(kernel, out_shape=(jax.ShapeDtypeStruct((1, 1), F32), jax....  173 us

profile of v1, /device:TPU:1, one launch (start us, length us, event | category | flops | bytes accessed | tf_op | source)
XLA Modules:
  0.0 179.0 jit_solution(12584750097990417290)
XLA Ops:
  0.6 173.4 %towers_step.1 = (f32[1,1]{1,0:T(1,128)}, f32[96,560]{1,0:T(8,128)}, f32[96,96]{1,0:T(8,128)}) custom-call(bf16[96,1536]{1,0:T(8,128)(2,1)} %qa.1, bf16[1536]{0:T(1024)(128)(2,1)} %qg.1, bf16[560,1536]{1,0:T(8,128)(2,1)} %bitcast.7, bf16[560,1536]{1,0:T(8,128)(2,1)} %bitcast.8, bf16[560,1536]{1,0:T(8,128)(2,1)} %down_hbm.1, bf16[32,768]{1,0:T(8,128)(2,1)} %ia.1, ...), custom_call_target="tpu_custom_call" | custom-call | tf_op jit(solution)/shard_map/towers_step/pallas_call | solution.py:981
  174.0 1.5 copy.18
  176.2 1.7 copy.22

commit v2 on v0

--- a/solution.py
+++ b/solution.py
@@ -313,10 +313,10 @@
 def kernel(
     qa, qg, gate_hbm, up_hbm, down_hbm, ia, ig, ig_w, iu_w, id_w, qf, if_, proj_hbm, ranks, positive,
     loss, q_out, i_out,
-    w, proj, nq, part, gate_val, h2, pm, r1, r2, zs, zin, ni, wi, ip, land, hq, hi,
-    sums, hats, scal, yq, grad, yi, gq, gi, qc1, qb1, qb2, qc, ic1, ib1, ib2, ic,
+    w, stage, proj, nq, part, gate_val, h2, pm, r1, r2, zs, zin, ni, wi, ip, land, hq, hi,
+    sums, hats, scal, yq, hw, yi, gq, gi, qc1, qb1, qb2, qc, ic1, ib1, ib2, ic,
     loads, gs, gr, ss, sr, ws, wr, vs, vr, hs, hr, ias, iar, irs, irr,
-    s1, r1s, s2, r2s, s3, r3s, ys, yr, iys, iyr, qs, qv, bs, bv,
+    s1, s2, s3, ys, yr, iys, iyr, qs, qv, bs, bv,
 ):
     p = Place()
     n, dq = qa.shape
@@ -349,8 +349,14 @@
         return {"dp": other // 2, "tower": other % 2}
 
     own_weights = [
-        pltpu.make_async_copy(ref, w.at[0, index, pl.ds(0, f), :], loads.at[index])
-        for index, ref in enumerate((gate_hbm, up_hbm, down_hbm))
+        pltpu.make_async_copy(ref, dst, loads.at[index])
+        for index, (ref, dst) in enumerate(
+            (
+                (gate_hbm, w.at[0, 0, pl.ds(0, f), :]),
+                (up_hbm, w.at[0, 1, pl.ds(0, f), :]),
+                (down_hbm, stage),
+            )
+        )
     ]
     proj_copy = pltpu.make_async_copy(proj_hbm, proj, loads.at[3])
     for copy in own_weights:
@@ -422,25 +428,36 @@
 
     def w_near(index):
         w_got(index, 0)
-        for kind in (1, 2, 5):
+        for kind in (1, 2, 5) if index == 2 else (1, 2):
             w_send(index, kind).start()
 
     def w_ring(index):
         w_got(index, 1)
         w_send(index, 3).start()
-        w_send(index, 6).start()
         w_got(index, 2)
         w_send(index, 4).start()
-        w_send(index, 7).start()
+        if index == 2:
+            w_send(index, 6).start()
+            w_send(index, 7).start()
 
     def w_far(index):
         w_got(index, 3)
         w_got(index, 4)
-        w_send(index, 8).start()
+        if index == 2:
+            w_send(index, 8).start()
+        else:
+            w_column(index, c).start()
+
+    def w_column(index, core):
+        ref = w.at[1, index, :, pl.ds(pl.multiple_of(core * wide, wide), wide)]
+        return remote(ref, ref, ws.at[8, index], wr.at[8, index], to_core)
 
     def w_done(index):
-        for kind in (5, 6, 7, 8):
-            w_got(index, kind)
+        if index < 2:
+            w_column(index, 1 - c).wait_recv()
+        else:
+            for kind in (5, 6, 7, 8):
+                w_got(index, kind)
 
     def vpiece(b, core):
         column = pl.multiple_of(core * (di // 2), di // 2)
@@ -579,6 +596,11 @@
     v_send(1).start()
     own_weights[1].wait()
     own_weights[2].wait()
+    for first_row in range(0, f, 112):
+        chunk = stage[first_row : first_row + 112, :]
+        for tower in range(2):
+            columns = slice(tower * wide, (tower + 1) * wide)
+            w[0, 2, first_row : first_row + 112, columns] = by_tower(chunk, count, tower)
     rows.take_x(0)
     item_hop(1)
     w_near(0)
@@ -622,55 +644,16 @@
     w_far(2)
     mate_up(0)
     w_done(2)
-    mate_down(1, 0)
-    mate_down(1, 1)
-    combine(1, 0)
-    mate_down(0, 0)
-    combine(1, 1)
-    mate_down(0, 1)
-    isum_hop(3)
-    send_sum(0)
-    combine(0, 0)
-    send_sum(1)
-    combine(0, 1)
-    isum.take(4)
-    own_item = ip[pl.ds(pl.multiple_of(p.z * m, m), m), :].astype(F32)
-    i_resid = ia[...].astype(F32) + (own_item + land[0, 3].astype(F32) + land[1, 3].astype(F32))
-    mlp = []
-    for q in range(2):
-        total = summed(0, q)
-        to_owner(q).wait_recv()
-        mlp.append(total + zin[q].astype(F32))
-    q_resid = qa[...].astype(F32) + jnp.concatenate(mlp, axis=1)
-
-    q_gain, i_gain = gain_row(qf), gain_row(if_)
-    q_scale, i_scale = rms_scale(q_resid), rms_scale(i_resid)
-    sums[p.t, :, :dq] = jnp.sum(q_resid * q_scale * q_gain, axis=0, keepdims=True)
-    sums[p.t, :, dq:] = jnp.sum(i_resid * i_scale * i_gain, axis=0, keepdims=True)
-
-    def spread_members(buf, send, recv):
-        def each(step, _):
-            remote(buf.at[p.t], buf.at[p.t], send.at[step], recv.at[p.t], member(step)).start()
+    def spread(buf, mine, sems, partner):
+        def each(hop, _):
+            remote(buf.at[mine], buf.at[mine], sems.at[0], sems.at[1], partner(hop)).start()
             return 0
 
-        lax.fori_loop(1, parts, each, 0)
-
-    def await_members(buf, send, recv):
-        def each(step, _):
-            other = (p.t + step) % parts
-            remote(buf.at[p.t], buf.at[other], send.at[step], recv.at[other], member(step)).wait()
-            return 0
-
-        lax.fori_loop(1, parts, each, 0)
-
-    def spread_hats(step, _):
-        remote(hats.at[own], hats.at[own], s2.at[step], r2s.at[own], replica(step)).start()
-        return 0
-
-    def gathered_hats(step, _):
-        other = (own + step) % count
-        remote(hats.at[own], hats.at[other], s2.at[step], r2s.at[other], replica(step)).wait()
-        return 0
+        lax.fori_loop(1, buf.shape[0], each, 0)
+
+    def gathered(buf, sems):
+        ref = buf.at[pl.ds(0, buf.shape[0] - 1)]
+        remote(ref, ref, sems.at[0], sems.at[1], member(1)).wait()
 
     def q_rows(tower, line_of, core):
         return rows_of(gq.at[tower], (line_of * 2 + core) * block_wide, block_wide, block_wide)
@@ -798,53 +781,102 @@
     gather = [RowGather(p, yq.at[tower], n, ys.at[tower], yr.at[tower]) for tower in range(2)]
     igather = RingGather(p, yi, m, iys, iyr)
 
-    def take_z(g):
-        gather[g // ZL].take_z(p.order(g % ZL))
-
-    def take_x(g):
-        gather[g // ZL].take_x(p.order(g % ZL))
+    steps = (0, 1, 4, 2, 3, 5, 6, 7)
+
+    def advance(index):
+        if index < len(steps):
+            g = steps[index]
+            gather[g // ZL].take_z(p.order(g % ZL))
+        if 0 <= index - 2 < len(steps):
+            g = steps[index - 2]
+            gather[g // ZL].take_x(p.order(g % ZL))
 
     def item_grad_hop(hop):
         igather.take(hop)
         if hop < 4:
             igather.start(hop + 1)
 
-    def product(g):
-        tower = g // ZL
-        s = p.order(g % ZL)
-        gather[tower].take_halves(s)
-        for b in range(X):
-            tile = scal[s * X + b]
-            columns = jnp.concatenate([tile] * 16, axis=0).T[:n]
-            first_row = pl.multiple_of((s * X + b) * n, n)
-            resid = yq[tower, pl.ds(first_row, n), :].astype(F32)
-            value = columns[:, 0:1] * along_of[tower] - resid * columns[:, 1:2]
-            grad[b * n : (b + 1) * n, :] = value.astype(BF16)
-        here = pl.ds(pl.multiple_of(s * group, group), group)
-        value = dot(grad[...], hq[here, :], ((0,), (0,)))
-        gq[tower] = value if g % ZL == 0 else gq[tower] + value
-
-    spread_members(sums, s1, r1s)
+    def scale_hidden():
+        line = lax.broadcasted_iota(jnp.int32, (128, 128), 0)
+        tiles = [jnp.zeros((128, 128), F32)] * 2
+        for t in range(parts):
+            for kind in range(2):
+                tiles[kind] = jnp.where(line == t, scal[t, kind : kind + 1, :], tiles[kind])
+        scale_of, slope_of = tiles[0].T[:n], tiles[1].T[:n]
+        total = jnp.zeros((1, f), F32)
+        for t in range(parts):
+            here = slice(t * n, (t + 1) * n)
+            value = hq[here, :].astype(F32)
+            hw[here, :] = (value * slope_of[:, t : t + 1]).astype(BF16)
+            total = total + jnp.sum(value * scale_of[:, t : t + 1], axis=0, keepdims=True)
+        return total
+
+    def product(tower, part_of):
+        total = 0.0
+        for j in (2 * part_of, 2 * part_of + 1):
+            s = p.order(j)
+            gather[tower].take_halves(s)
+            here = pl.ds(pl.multiple_of(s * group, group), group)
+            total = total + dot(yq[tower, here, :], hw[here, :], ((0,), (0,)))
+        if part_of == 0:
+            column = jnp.broadcast_to(along_of[tower], (128, wide)).T[:, 0:1]
+            gq[tower] = column * summed_hidden - total
+        else:
+            gq[tower] -= total
+
+    def resid_half(tower):
+        total = summed(0, tower)
+        to_owner(tower).wait_recv()
+        total = total + zin[tower].astype(F32)
+        value = by_tower(qa[...], count, tower).astype(F32) + total
+        yq[tower, pl.ds(pl.multiple_of(p.t * n, n), n), :] = value.astype(BF16)
+        return value
+
+    mate_down(1, 0)
+    mate_down(0, 0)
+    combine(1, 0)
+    mate_down(1, 1)
+    combine(0, 0)
+    mate_down(0, 1)
+    send_sum(0)
+    combine(1, 1)
+    combine(0, 1)
+    isum_hop(3)
+    send_sum(1)
+    q_resid = [resid_half(0)]
+    advance(0)
+    isum.take(4)
+    own_item = ip[pl.ds(pl.multiple_of(p.z * m, m), m), :].astype(F32)
+    i_resid = ia[...].astype(F32) + (own_item + land[0, 3].astype(F32) + land[1, 3].astype(F32))
+    i_gain = gain_row(if_)
+    i_scale = rms_scale(i_resid)
+    sums[p.t, :, dq:] = jnp.sum(i_resid * i_scale * i_gain, axis=0, keepdims=True)
+    q_gain = gain_row(qf)
+    gain_of = [by_tower(q_gain, count, tower) for tower in range(2)]
+    advance(1)
+    q_resid.append(resid_half(1))
+    square = sum(jnp.sum(value * value, axis=-1, keepdims=True) for value in q_resid)
+    q_scale = lax.rsqrt(square / dq + EPS)
     for tower in range(2):
-        here = pl.ds(pl.multiple_of(p.t * n, n), n)
-        yq[tower, here, :] = by_tower(q_resid, count, tower).astype(BF16)
-    take_z(0)
+        part_sum = jnp.sum(q_resid[tower] * q_scale * gain_of[tower], axis=0, keepdims=True)
+        sums[p.t, :, tower * wide : (tower + 1) * wide] = part_sum
+    spread(sums, p.t, s1, member)
+    advance(2)
     proj_copy.wait()
-    await_members(sums, s1, r1s)
+    gathered(sums, s1)
     total = sums[0]
     for slot in range(1, parts):
         total = total + sums[slot]
-    q_pooled = total[:, :dq] / QLEN
+    firsts = [(d % 2) * wide + (d // 2) * block_wide for d in range(count)]
+    q_pooled = jnp.concatenate([total[:, at : at + block_wide] for at in firsts], axis=1) / QLEN
     i_pooled = total[:, dq:] / ILEN
     q_e = jnp.sum(dot(split_rows(q_pooled), proj[...]), axis=0, keepdims=True)
     q_norm, i_norm = unit_scale(q_e), unit_scale(i_pooled)
     hats[own, :, :di] = q_e * q_norm
     hats[own, :, di:] = i_pooled * i_norm
-    lax.fori_loop(1, count, spread_hats, 0)
-    take_z(1)
-    take_z(4)
-    take_x(0)
-    lax.fori_loop(1, count, gathered_hats, 0)
+    spread(hats, own, s2, replica)
+    advance(3)
+    gathered(hats, s2)
     index = lax.broadcasted_iota(jnp.int32, (count, 2 * di), 0)
     every = jnp.zeros((count, 2 * di), F32)
     for slot in range(count):
@@ -857,8 +889,7 @@
     per_row, slopes = contrast(every_query, every_items, ranks[...], target)
     loss[...] = jnp.sum(per_row, axis=0, keepdims=True) / count
     weights = slopes * (LOSS_SCALE / (TAU * count))
-    take_z(2)
-    take_x(1)
+    advance(4)
     mine = lax.broadcasted_iota(jnp.int32, (count, di), 0) == own
     q_back = jnp.sum(
         jnp.where(mine, dot(weights, every_items, precision=HIGH), 0.0), axis=0, keepdims=True
@@ -869,59 +900,54 @@
         axis=0,
         keepdims=True,
     )
+    advance(5)
     q_grad_e = unit_back(q_e, q_norm, q_back)
     q_up = jnp.sum(dot(split_rows(q_grad_e), proj[...], ((1,), (1,))), axis=0, keepdims=True) / QLEN
     i_up = unit_back(i_pooled, i_norm, i_back) / ILEN
     along = q_gain * q_up
     along_of = [by_tower(along, count, tower) for tower in range(2)]
-    inner = jnp.mean(along * q_resid, axis=-1, keepdims=True)
+    inner = sum(
+        jnp.sum(along_of[tower] * q_resid[tower], axis=-1, keepdims=True) for tower in range(2)
+    )
+    inner = inner / dq
     slope = (q_scale * q_scale * q_scale) * inner
     lane = lax.broadcasted_iota(jnp.int32, (n, 128), 1)
     columns = jnp.where(lane == 0, q_scale, jnp.where(lane == 1, slope, 0.0))
     columns = jnp.concatenate([columns, jnp.zeros((128 - n, 128), F32)], axis=0)
     scal[p.t] = columns.T[:8]
-    spread_members(scal, s3, r3s)
+    spread(scal, p.t, s3, member)
     yi[pl.ds(pl.multiple_of(p.z * m, m), m), :] = grad_rows(i_resid, i_scale, i_gain, i_up)
     igather.start(1)
-    take_z(3)
-    take_x(4)
-    item_grad_hop(1)
-    await_members(scal, s3, r3s)
+    advance(6)
+    gathered(scal, s3)
     back_got(0)
     back_got(1)
-    product(0)
-    take_z(5)
-    take_x(2)
-    product(1)
+    summed_hidden = scale_hidden()
+    advance(7)
+    item_grad_hop(1)
+    product(0, 0)
+    advance(8)
     item_grad_hop(2)
-    take_z(6)
-    take_x(3)
-    product(2)
-    take_z(7)
+    product(0, 1)
+    q_start(0)
+    advance(9)
     item_grad_hop(3)
-    product(3)
-    q_start(0)
-    take_x(5)
     q_far(0)
-    product(4)
+    product(1, 0)
     item_grad_hop(4)
-    take_x(6)
     q_near(0)
+    product(1, 1)
+    q_start(1)
     i_product()
-    product(5)
-    take_x(7)
+    q_far(1)
+    q_own(0)
     i_far()
-    product(6)
-    q_own(0)
+    q_near(1)
     i_near()
-    product(7)
-    q_start(1)
-    q_far(1)
+    q_own(1)
     i_own()
-    q_near(1)
+    q_finish(0)
     i_finish()
-    q_finish(0)
-    q_own(1)
     q_finish(1)
 
     for j in range(2):
@@ -938,8 +964,10 @@
     items.drain()
     isum.drain()
     for index in range(3):
-        for kind in range(9):
+        for kind in range(9) if index == 2 else range(5):
             w_send(index, kind).wait_send()
+    for index in range(2):
+        w_column(index, c).wait_send()
     for kind in range(7):
         v_send(kind).wait_send()
     for tower in range(2):
@@ -988,6 +1016,7 @@
         out_specs=[vmem] * 3,
         scratch_shapes=[
             pltpu.VMEM((2, 3, padded, dq), BF16),
+            pltpu.VMEM(down.shape, BF16),
             pltpu.VMEM(proj.shape, BF16),
             pltpu.VMEM((2 * group, dq), BF16),
             pltpu.VMEM((2, group, dq), F32),
@@ -1008,7 +1037,7 @@
             pltpu.VMEM((count, 1, 2 * di), F32),
             pltpu.VMEM((parts, 8, 128), F32),
             pltpu.VMEM((2, parts * n, dq // 2), BF16),
-            pltpu.VMEM((group, dq // 2), BF16),
+            pltpu.VMEM((ZL * group, f), BF16),
             pltpu.VMEM((all_i, di), BF16),
             pltpu.VMEM((2, dq // 2, f), F32),
             pltpu.VMEM((X, di, k), F32),
@@ -1035,12 +1064,9 @@
             dma((2, 4)),
             dma((2, 4)),
             dma((2, 4)),
-            dma((parts,)),
-            dma((parts,)),
-            dma((count,)),
-            dma((count,)),
-            dma((parts,)),
-            dma((parts,)),
+            dma((2,)),
+            dma((2,)),
+            dma((2,)),
             dma((2, 6, ZL)),
             dma((2, 5, ZL)),
             dma((2, 4)),

time: 178 us -> 175 us (0.983); the launches traced: 177 us -> 171 us
  Pallas kernels: 171 us -> 166 us
    pallas_call x1, Pallas kernels: 171 us -> 166 us  [step(): pl.pallas_call(kernel, out_shape=(jax.ShapeDtypeStruct((1, 1), F32), jax....]
where the time goes in v2:
time: 175 us; the launch traced here: 171 us
  Pallas kernels  166 us (95%)
  local copies, waits for them, and re-layouts  3.16 us (2%)
  between operations  2.47 us (1%)
    pallas_call x1, Pallas kernels, step(): pl.pallas_call(kernel, out_shape=(jax.ShapeDtypeStruct((1, 1), F32), jax....  166 us

profile of v2, /device:TPU:1, one launch (start us, length us, event | category | flops | bytes accessed | tf_op | source)
XLA Modules:
  0.0 171.4 jit_solution(10432868905776665258)
XLA Ops:
  0.6 165.8 %towers_step.1 = (f32[1,1]{1,0:T(1,128)}, f32[96,560]{1,0:T(8,128)}, f32[96,96]{1,0:T(8,128)}) custom-call(bf16[96,1536]{1,0:T(8,128)(2,1)} %qa.1, bf16[1536]{0:T(1024)(128)(2,1)} %qg.1, bf16[560,1536]{1,0:T(8,128)(2,1)} %bitcast.7, bf16[560,1536]{1,0:T(8,128)(2,1)} %bitcast.8, bf16[560,1536]{1,0:T(8,128)(2,1)} %down_hbm.1, bf16[32,768]{1,0:T(8,128)(2,1)} %ia.1, ...), custom_call_target="tpu_custom_call" | custom-call | tf_op jit(solution)/shard_map/towers_step/pallas_call | solution.py:1008
  166.4 1.5 copy.18
  168.6 1.7 copy.22

commit v3 on v2

--- a/solution.py
+++ b/solution.py
@@ -864,6 +864,7 @@
     advance(2)
     proj_copy.wait()
     gathered(sums, s1)
+    advance(3)
     total = sums[0]
     for slot in range(1, parts):
         total = total + sums[slot]
@@ -875,7 +876,7 @@
     hats[own, :, :di] = q_e * q_norm
     hats[own, :, di:] = i_pooled * i_norm
     spread(hats, own, s2, replica)
-    advance(3)
+    advance(4)
     gathered(hats, s2)
     index = lax.broadcasted_iota(jnp.int32, (count, 2 * di), 0)
     every = jnp.zeros((count, 2 * di), F32)
@@ -887,9 +888,9 @@
     for slot in range(count):
         target = jnp.where(line == slot, positive[slot], target)
     per_row, slopes = contrast(every_query, every_items, ranks[...], target)
+    advance(5)
     loss[...] = jnp.sum(per_row, axis=0, keepdims=True) / count
     weights = slopes * (LOSS_SCALE / (TAU * count))
-    advance(4)
     mine = lax.broadcasted_iota(jnp.int32, (count, di), 0) == own
     q_back = jnp.sum(
         jnp.where(mine, dot(weights, every_items, precision=HIGH), 0.0), axis=0, keepdims=True
@@ -900,10 +901,11 @@
         axis=0,
         keepdims=True,
     )
-    advance(5)
+    advance(6)
     q_grad_e = unit_back(q_e, q_norm, q_back)
     q_up = jnp.sum(dot(split_rows(q_grad_e), proj[...], ((1,), (1,))), axis=0, keepdims=True) / QLEN
     i_up = unit_back(i_pooled, i_norm, i_back) / ILEN
+    advance(7)
     along = q_gain * q_up
     along_of = [by_tower(along, count, tower) for tower in range(2)]
     inner = sum(
@@ -918,22 +920,20 @@
     spread(scal, p.t, s3, member)
     yi[pl.ds(pl.multiple_of(p.z * m, m), m), :] = grad_rows(i_resid, i_scale, i_gain, i_up)
     igather.start(1)
-    advance(6)
     gathered(scal, s3)
+    advance(8)
     back_got(0)
     back_got(1)
     summed_hidden = scale_hidden()
-    advance(7)
+    advance(9)
     item_grad_hop(1)
     product(0, 0)
-    advance(8)
     item_grad_hop(2)
     product(0, 1)
     q_start(0)
-    advance(9)
     item_grad_hop(3)
+    product(1, 0)
     q_far(0)
-    product(1, 0)
     item_grad_hop(4)
     q_near(0)
     product(1, 1)

time: 175 us -> 181 us (1.034); the launches traced: 171 us -> 180 us
  Pallas kernels: 166 us -> 174 us
    pallas_call x1, Pallas kernels: 166 us -> 174 us  [step(): pl.pallas_call(kernel, out_shape=(jax.ShapeDtypeStruct((1, 1), F32), jax....]
where the time goes in v3:
time: 181 us; the launch traced here: 180 us
  Pallas kernels  174 us (96%)
  local copies, waits for them, and re-layouts  3.16 us (2%)
  between operations  2.47 us (1%)
    pallas_call x1, Pallas kernels, step(): pl.pallas_call(kernel, out_shape=(jax.ShapeDtypeStruct((1, 1), F32), jax....  174 us

profile of v3, /device:TPU:1, one launch (start us, length us, event | category | flops | bytes accessed | tf_op | source)
XLA Modules:
  0.0 179.8 jit_solution(9074629864701382024)
XLA Ops:
  0.6 174.2 %towers_step.1 = (f32[1,1]{1,0:T(1,128)}, f32[96,560]{1,0:T(8,128)}, f32[96,96]{1,0:T(8,128)}) custom-call(bf16[96,1536]{1,0:T(8,128)(2,1)} %qa.1, bf16[1536]{0:T(1024)(128)(2,1)} %qg.1, bf16[560,1536]{1,0:T(8,128)(2,1)} %bitcast.7, bf16[560,1536]{1,0:T(8,128)(2,1)} %bitcast.8, bf16[560,1536]{1,0:T(8,128)(2,1)} %down_hbm.1, bf16[32,768]{1,0:T(8,128)(2,1)} %ia.1, ...), custom_call_target="tpu_custom_call" | custom-call | tf_op jit(solution)/shard_map/towers_step/pallas_call | solution.py:1008
  174.9 1.5 copy.18
  177.1 1.7 copy.22
